TPU v7x, 256 devices: a whole 4x4x8 slice. The times are simulated.
256 devices in a mesh: grp: 8 (over x_hi, y), blk: 32 (over z, x_lo, core).
Axes of the slice: x: 4 (x_hi: 2, x_lo: 2; x = x_hi * 2 + x_lo), y: 4, z: 8, core: 2. Of those that a mesh axis runs over, the one named last changes fastest.
Arguments:
- residual_in: bfloat16 [512, 16384], P('grp', 'blk'), may hold values from -6 to 6
- queries: bfloat16 [512, 16384], P('grp')
- key_cache: bfloat16 [512, 32, 64, 128], P('grp', 'blk')
- value_cache: bfloat16 [512, 32, 64, 128], P('grp', 'blk'), may hold values from -6 to 6
- key_new: bfloat16 [512, 1024], P('grp'), may hold values from -6 to 6
- value_new: bfloat16 [512, 1024], P('grp'), may hold values from -6 to 6
- lengths: int32 [512], P('grp'), may hold values from 2 to 256, as said below
- ffn_gain: bfloat16 [16384], P('blk'), may hold values from 0.099609375 to 1.8984375
- gate_weight: bfloat16 [16384, 26624], P('blk', 'grp'), may hold values from -0.046875 to 0.046875
- up_weight: bfloat16 [16384, 26624], P('blk', 'grp'), may hold values from -0.046875 to 0.046875
- down_weight: bfloat16 [26624, 16384], P('grp', 'blk'), may hold values from -0.0390625 to 0.0390625
Outputs:
- layer_out: float32 [512, 16384], P('grp', 'blk')
Inputs may be any that keep to these rules, and one draw needn't show every extreme that they name: `lengths`: every sequence has at least two valid cache positions, and some sequence fills all 256.
All inputs are finite; a program needn't handle non-finite values.
Results may differ from a plain program's by a relative error of at most 0.0075.
Values may be sent and summed in bfloat16 or wider, within the bound.
A program may use at most 128 MiB of HBM per device.

v0:
```python
import math

import jax
import jax.numpy as jnp
from jax import lax
from jax.sharding import PartitionSpec as P

D = 16384
HEADS = 128
KV_HEADS = 8


def partner(x, axis, distance):
    return lax.ppermute(x, axis, [(i, i ^ 1 << distance) for i in range(lax.axis_size(axis))])


def on_device(
    residual_in,
    queries,
    key_cache,
    value_cache,
    key_new,
    value_new,
    lengths,
    ffn_gain,
    gate_weight,
    up_weight,
    down_weight,
):
    cycle_size = lax.axis_size("blk")
    quarters = cycle_size // KV_HEADS
    per_kv = HEADS // KV_HEADS
    own_heads = HEADS // cycle_size
    head_size = key_cache.shape[3]
    seq_rows = residual_in.shape[0]
    positions_here = key_cache.shape[2]
    blk_index = lax.axis_index("blk")
    kv_head = blk_index // quarters
    quarter = blk_index % quarters
    score_scale = 1.0 / math.sqrt(head_size)
    group_queries = lax.dynamic_slice_in_dim(
        queries, kv_head * per_kv * head_size, per_kv * head_size, 1
    )
    group_queries = group_queries.astype(jnp.float32).reshape(seq_rows, per_kv, head_size)
    fresh_key = lax.dynamic_slice_in_dim(key_new, kv_head * head_size, head_size, 1).astype(
        jnp.float32
    )
    fresh_value = lax.dynamic_slice_in_dim(value_new, kv_head * head_size, head_size, 1).astype(
        jnp.float32
    )
    keys_here = key_cache[:, 0].astype(jnp.float32)
    values_here = value_cache[:, 0].astype(jnp.float32)
    scores = jnp.einsum("shd,spd->shp", group_queries, keys_here) * score_scale
    fresh_scores = jnp.einsum("shd,sd->sh", group_queries, fresh_key) * score_scale
    places = quarter * positions_here + jnp.arange(positions_here, dtype=jnp.int32)
    usable = (places[None, :] < lengths[:, None])[:, None, :]
    with_fresh = quarter == 0
    largest = jnp.maximum(
        jnp.max(jnp.where(usable, scores, -1e30), axis=2),
        jnp.where(with_fresh, fresh_scores, -1e30),
    )
    weights = jnp.where(usable, jnp.exp(scores - largest[..., None]), 0.0)
    fresh_weight = jnp.where(with_fresh, jnp.exp(fresh_scores - largest), 0.0)
    totals = jnp.sum(weights, axis=2) + fresh_weight
    weighted = (
        jnp.einsum("shp,spd->shd", weights, values_here)
        + fresh_weight[..., None] * fresh_value[:, None, :]
    )
    for bit_number in range(quarters.bit_length() - 1):
        peer_max, peer_total, peer_weighted = partner(
            (largest, totals, weighted), "blk", bit_number
        )
        merged = jnp.maximum(largest, peer_max)
        mine_factor = jnp.exp(largest - merged)
        peer_factor = jnp.exp(peer_max - merged)
        totals = totals * mine_factor + peer_total * peer_factor
        weighted = weighted * mine_factor[..., None] + peer_weighted * peer_factor[..., None]
        largest = merged
    attention = weighted / totals[..., None]
    own_output = lax.dynamic_slice_in_dim(attention, quarter * own_heads, own_heads, 1).reshape(
        seq_rows, own_heads * head_size
    )
    wide = residual_in.astype(jnp.float32) + own_output
    row_total = lax.psum(jnp.sum(wide * wide, axis=1), "blk")
    inverse = lax.rsqrt(row_total / D + 1e-05)
    normed = (wide * ffn_gain.astype(jnp.float32)[None, :] * inverse[:, None]).astype(jnp.bfloat16)
    piece = lax.all_gather(normed, "grp", axis=0, tiled=True)
    gate_part = jnp.dot(piece, gate_weight, preferred_element_type=jnp.float32)
    up_part = jnp.dot(piece, up_weight, preferred_element_type=jnp.float32)
    partial_sums = jnp.stack([gate_part, up_part], axis=1)
    summed = lax.psum(partial_sums, "blk")
    hidden = (jax.nn.silu(summed[:, 0]) * summed[:, 1]).astype(jnp.bfloat16)
    down_terms = jnp.dot(hidden, down_weight, preferred_element_type=jnp.float32)
    returned = lax.psum_scatter(down_terms, "grp", scatter_dimension=0, tiled=True)
    return wide + returned


def solution(mesh):
    in_specs = (
        P("grp", "blk"),
        P("grp", None),
        P("grp", "blk", None, None),
        P("grp", "blk", None, None),
        P("grp", None),
        P("grp", None),
        P("grp"),
        P("blk"),
        P("blk", "grp"),
        P("blk", "grp"),
        P("grp", "blk"),
    )
    out_specs = P("grp", "blk")
    return jax.shard_map(
        on_device, mesh=mesh, in_specs=in_specs, out_specs=out_specs, check_vma=False
    )
```

profile of v0, /device:TPU:7, one launch (start us, length us, event | category | flops | bytes accessed | tf_op | source)
XLA Modules:
  0.0 554.1 jit_solution(16960927538323434149)
XLA Ops:
  6.6 0.9 dynamic-slice_bitcast_fusion.1
  7.4 0.9 dynamic-slice_convert_fusion
  8.3 1.0 dynamic-slice_bitcast_fusion
  9.3 0.7 broadcast_compare_fusion
  10.1 0.2 fusion.15
  10.3 2.0 select_reduce_fusion
  12.3 0.4 fusion.6
  12.7 1.7 convolution_add_fusion
  14.4 0.8 collective-permute-start.1
  15.1 0.1 collective-permute-start.4
  15.2 0.4 collective-permute-start
  15.7 1.1 collective-permute-done.4
  16.8 1.1 multiply_add_fusion
  17.9 0.5 collective-permute-start.3
  18.5 0.9 collective-permute-start.5
  19.4 0.6 collective-permute-start.2
  20.0 12.1 %collective-permute-done.5 = f32[64,16]{1,0:T(8,128)S(1)} collective-permute-done((f32[64,16]{1,0:T(8,128)S(1)}, f32[64,16]{1,0:T(8,128)S(1)}, u32[]{:S(2)}, u32[]{:S(2)}) %collective-permute-start.5) | collective-permute-done | bytes 4128 | tf_op jit(solution)/shard_map/ppermute | solution.py:14
  32.1 0.7 collective-permute-done.2
  32.8 0.1 constant_dynamic-slice_fusion.2
  32.9 0.1 constant_dynamic-slice_fusion
  33.0 1.3 fusion.11
  34.3 1.0 multiply_reduce_fusion
  35.3 52.6 %psum.14 = f32[64]{0:T(128)S(1)} all-reduce(f32[64]{0:T(128)S(1)} %multiply_reduce_fusion), channel_id=1, replica_groups=mesh['grp'=8,'blk'=32] {'blk'}, use_global_device_ids=true, to_apply=%region_3.4 | all-reduce | flops 64 | bytes 512 | tf_op jit(solution)/shard_map/psum | solution.py:84
  87.9 1.1 multiply_convert_fusion
  89.0 29.1 %all_gather.3 = bf16[512,512]{1,0:T(8,128)(2,1)S(1)} all-gather(bf16[64,512]{1,0:T(8,128)(2,1)S(1)} %multiply_convert_fusion), channel_id=1, replica_groups=mesh['grp'=8,'blk'=32] {'grp'}, dimensions={0}, use_global_device_ids=true | all-gather | bytes 589824 | tf_op jit(solution)/shard_map/all_gather | solution.py:87
  118.1 4.7 convolution_bitcast_fusion
  122.8 4.7 convolution_bitcast_fusion.1
  127.5 10.6 %pad_maximum_fusion = f32[512,2,3328]{2,0,1:T(8,128)} fusion(f32[512,1,3328]{2,0,1:T(8,128)} %convolution_bitcast_fusion, f32[512,1,3328]{2,0,1:T(8,128)} %convolution_bitcast_fusion.1), kind=kLoop, calls=%fused_computation | loop fusion | flops 3407872 | bytes 27262976 | tf_op jit(solution)/shard_map/stack | solution.py:90
  138.2 322.5 %all-reduce.2.cloned.1.call-done = f32[512,2,3328]{2,0,1:T(8,128)} async-done(((f32[512,2,3328]{2,0,1:T(8,128)}), f32[512,2,3328]{2,0,1:T(8,128)}) %all-reduce.2.cloned.1.call-update) | async-done | bytes 13631504 | tf_op jit(solution)/shard_map/psum | solution.py:91
  460.7 8.7 %fusion.2 = f32[512,512]{1,0:T(8,128)} fusion(bf16[3328,512]{1,0:T(8,128)(2,1)} %param.21, f32[512,2,3328]{2,0,1:T(8,128)} %all-reduce.2.cloned.1.call-done), kind=kOutput, calls=%fused_computation.7 | convolution fusion | flops 1755054080 | bytes 18087936 | tf_op jit(solution)/shard_map/dot_general | solution.py:93
  469.4 76.2 %reduce-scatter.2.cloned.1.call-done = f32[64,512]{1,0:T(8,128)} async-done(((f32[512,512]{1,0:T(8,128)}), f32[64,512]{1,0:T(8,128)}) %reduce-scatter.2.cloned.1.call-update) | async-done | bytes 131088 | tf_op jit(solution)/shard_map/reduce_scatter | solution.py:94
  545.7 1.6 fusion.12
  (21 shorter events, 0.3 us)
Async XLA Ops:
  6.5 111.5 %copy-start = (bf16[512,3328]{1,0:T(8,128)(2,1)S(1)}, bf16[512,3328]{1,0:T(8,128)(2,1)}, u32[]{:S(2)}) copy-start(bf16[512,3328]{1,0:T(8,128)(2,1)} %param.20) | copy-start | bytes 10223620
  6.5 13.4 %copy-start.2 = (bf16[512]{0:T(512)(128)(2,1)S(1)}, bf16[512]{0:T(512)(128)(2,1)}, u32[]{:S(2)}) copy-start(bf16[512]{0:T(512)(128)(2,1)} %param.18) | copy-start | bytes 3076
  6.5 454.1 %all-reduce.2.cloned.1.call-start = ((), (), s32[]{:S(2)}) async-start(), calls=%async_computation.1 | async-start | bytes 27262976 | tf_op jit(solution)/shard_map/psum | solution.py:91
  14.4 2.4 collective-permute-start.1
  15.1 1.6 collective-permute-start.4
  15.2 1.5 collective-permute-start
  17.9 15.0 %collective-permute-start.3 = (f32[64,16,128]{2,1,0:T(8,128)}, f32[64,16,128]{2,1,0:T(8,128)}, u32[]{:S(2)}, u32[]{:S(2)}) collective-permute-start(f32[64,16,128]{2,1,0:T(8,128)} %multiply_add_fusion), channel_id=1, source_target_pairs={{0,2},{1,3},{2,0},{3,1},{4,6},{5,7},{6,4},{7,5},{8,10},{9,11},{10,... | collective-permute-start | bytes 1572872 | tf_op jit(solution)/shard_map/ppermute | solution.py:14
  18.5 13.6 %collective-permute-start.5 = (f32[64,16]{1,0:T(8,128)S(1)}, f32[64,16]{1,0:T(8,128)S(1)}, u32[]{:S(2)}, u32[]{:S(2)}) collective-permute-start(f32[64,16]{1,0:T(8,128)S(1)} %get-tuple-element.8), channel_id=1, source_target_pairs={{0,2},{1,3},{2,0},{3,1},{4,6},{5,7},{6,4},{7,5},{8,10},{9,11},{10,... | collective-permute-start | bytes 12296 | tf_op jit(solution)/shard_map/ppermute | solution.py:14
  19.4 13.4 %collective-permute-start.2 = (f32[64,16]{1,0:T(8,128)S(1)}, f32[64,16]{1,0:T(8,128)S(1)}, u32[]{:S(2)}, u32[]{:S(2)}) collective-permute-start(f32[64,16]{1,0:T(8,128)S(1)} %get-tuple-element.11), channel_id=1, source_target_pairs={{0,2},{1,3},{2,0},{3,1},{4,6},{5,7},{6,4},{7,5},{8,10},{9,11},{10,... | collective-permute-start | bytes 12296 | tf_op jit(solution)/shard_map/ppermute | solution.py:14
  87.9 34.8 %copy-start.1 = (bf16[512,3328]{1,0:T(8,128)(2,1)S(1)}, bf16[512,3328]{1,0:T(8,128)(2,1)}, u32[]{:S(2)}) copy-start(bf16[512,3328]{1,0:T(8,128)(2,1)} %param.19) | copy-start | bytes 10223620
  138.2 407.5 %reduce-scatter.2.cloned.1.call-start = ((), (), s32[]{:S(2)}) async-start(), calls=%async_computation.2 | async-start | bytes 1179648 | tf_op jit(solution)/shard_map/reduce_scatter | solution.py:94
Sparse Core Ops, SparseCore 0:
  138.3 322.3 all-reduce.1
  469.6 76.0 reduce-scatter.1
where the time goes:
time: 557 us; the launch traced here: 554 us
  waiting for transfers between devices  413 us (74%)
  blocking collectives  81.7 us (15%)
  matrix products  22.1 us (4%)
  other arithmetic  18.7 us (3%)
  between operations  13.5 us (2%)
    psum x1, waiting for transfers between devices, on_device(): summed = lax.psum(partial_sums, 'blk')  322 us
    reduce_scatter x1, waiting for transfers between devices, on_device(): lax.psum_scatter(down_terms, 'grp', scatter_dimension=0, tiled=True)  76.2 us
    psum x1, blocking collectives, on_device(): row_total = lax.psum(jnp.sum(wide * wide, axis=1), 'blk')  52.6 us
    all_gather x1, blocking collectives, on_device(): piece = lax.all_gather(normed, 'grp', axis=0, tiled=True)  29.1 us
    ppermute x6, waiting for transfers between devices, partner(): lax.ppermute(x, axis, [(i, i ^ 1 << distance) for i in range(lax.axis_siz...  13.9 us
  transfers between devices with their start and end apart: 8, of which 5 were waited for; matrix products, arithmetic and copies ran while one was open for 0% of the time, Pallas kernels for 0%

commit v1 on v0

v1 whole, which is shorter than its diff:
```python
import functools
import math

import jax
import jax.numpy as jnp
from jax import lax
from jax.experimental import pallas as pl
from jax.experimental.pallas import tpu as pltpu
from jax.sharding import PartitionSpec as P

D = 16384
HEADS = 128
KV_HEADS = 8
MESH = pl.DeviceIdType.MESH
F32 = jnp.float32
BF16 = jnp.bfloat16

RING = 8
GROUPS = 8
FEAT = 512
HALF = 1664
WIDE = HALF + 128
C1 = 768
C2 = HALF - C1


def slot_of(distance):
    return jnp.where(distance <= 4, 8 - 2 * distance, 2 * distance - 9)


def kernel(
    w_in, st_in, res, gain, gate, up, down, out,
    w_got, st_got, wide_s, token_s, inv_gain,
    gate_w, up_w, down_w, x_s, pu, pg,
    xg_send, xg_recv, ua_send, ua_recv, ub_send, ub_recv,
    ga_send, ga_recv, gb_send, gb_recv, xu_send, xu_recv,
    h1, h2, dp, dr, ds_send, fr,
    local_sem, wsem_s, wsem_r, at_s, at_r, tok_s, tok_r, mate_s, mate_r,
    xg_ss, xg_rs, ua_ss, ua_rs, ub_ss, ub_rs, ga_ss, ga_rs, gb_ss, gb_rs, xu_ss, xu_rs,
    hz_s, hz_r, hx_s, hx_r, dr_s, dr_r, fr_s, fr_r,
):
    g = lax.axis_index("grp")
    b = lax.axis_index("blk")
    z = b // 4
    q = b % 4
    x = q // 2
    core = q % 2
    sign = 1 - 2 * core
    mate = (g, z * 4 + x * 2 + (1 - core))
    xmate = (g, z * 4 + (1 - x) * 2 + core)
    ahead = (g, lax.rem(z + sign + RING, RING) * 4 + q)
    behind = (g, lax.rem(z - sign + RING, RING) * 4 + q)
    x_other = 1 - x

    def remote(src, dst, ss, rs, to):
        return pltpu.make_async_remote_copy(
            src_ref=src, dst_ref=dst, send_sem=ss, recv_sem=rs, device_id=to, device_id_type=MESH
        )

    def peer(n):
        return (lax.rem(g // 4 + n // 4, 2)) * 4 + lax.rem(g % 4 + n % 4, 4)

    def source(n):
        return (lax.rem(g // 4 + n // 4, 2)) * 4 + lax.rem(g % 4 - n % 4 + 4, 4)

    ORDER = (1, 3, 2, 4, 5, 7, 6)

    mine = pl.ds(pl.multiple_of(core * HALF, 128), HALF)
    other = pl.ds(pl.multiple_of((1 - core) * HALF, 128), HALF)
    rows = pl.ds(pl.multiple_of(core * FEAT, FEAT), FEAT)
    loads = [
        pltpu.make_async_copy(gate.at[:, mine], gate_w.at[rows], local_sem.at[0]),
        pltpu.make_async_copy(up.at[:, mine], up_w.at[rows], local_sem.at[1]),
        pltpu.make_async_copy(down.at[mine], down_w.at[core], local_sem.at[2]),
    ]
    for load in loads:
        load.start()

    barrier = pltpu.get_barrier_semaphore()
    partners = [mate, xmate, (g, z * 4 + (1 - x) * 2 + (1 - core)), ahead, behind]
    partners += [(peer(n), b) for n in ORDER]
    for partner in partners:
        pl.semaphore_signal(barrier, inc=1, device_id=partner, device_id_type=MESH)

    inv_gain[core] = jnp.broadcast_to(1.0 / gain[...].astype(F32), (8, FEAT))
    pl.semaphore_wait(barrier, len(partners))

    merges = []
    for n in (3, 2, 1):
        p = q ^ n
        to = (g, z * 4 + p)
        merges.append(remote(st_in.at[p], st_got.at[q], at_s.at[n], at_r.at[q], to))
        merges.append(remote(w_in.at[p], w_got.at[q], at_s.at[4 + n], at_r.at[4 + q], to))
    for copy in merges:
        copy.start()
    pushes = [
        remote(inv_gain.at[core], inv_gain.at[core], wsem_s.at[0], wsem_r.at[0], mate),
        remote(up.at[:, other], up_w.at[rows], wsem_s.at[1], wsem_r.at[1], mate),
        remote(gate.at[:, other], gate_w.at[rows], wsem_s.at[2], wsem_r.at[2], mate),
        remote(down.at[other], down_w.at[core], wsem_s.at[3], wsem_r.at[3], mate),
    ]
    for push in pushes[:3]:
        push.start()
    st_got[q] = st_in[q]
    w_got[q] = w_in[q]
    for n in (1, 2, 3):
        p = q ^ n
        to = (g, z * 4 + p)
        remote(st_in.at[p], st_got.at[p], at_s.at[n], at_r.at[p], to).wait_recv()
        remote(w_in.at[p], w_got.at[p], at_s.at[4 + n], at_r.at[4 + p], to).wait_recv()
    for head in range(4):
        cols = slice(head * 128, head * 128 + 128)
        tops = [st_got[j][:, head : head + 1] for j in range(4)]
        sums = [st_got[j][:, 4 + head : 5 + head] for j in range(4)]
        top = jnp.maximum(jnp.maximum(tops[0], tops[1]), jnp.maximum(tops[2], tops[3]))
        factors = [jnp.exp(t - top) for t in tops]
        total = sum(f * s for f, s in zip(factors, sums))
        mixed = sum(f * w_got[j, :, cols].astype(F32) for j, f in enumerate(factors))
        wide = res[:, cols].astype(F32) + mixed / total
        wide_s[:, cols] = wide
        scaled = (wide * gain[:, cols].astype(F32)).astype(BF16)
        token_s[0, :, cols] = scaled[:32]
        token_s[1, :, cols] = scaled[32:]

    def slots(owner):
        away = lax.rem((owner - z) * sign + 2 * RING - 1, RING) + 1
        back = lax.rem(RING - away + RING - 1, RING) + 1
        return slot_of(away), slot_of(back)

    lanes = pl.ds(pl.multiple_of(core * FEAT, FEAT), FEAT)
    own_slot, own_mate_slot = slots(g)
    gathers = []
    for n in ORDER[::-1]:
        gathers.append(
            remote(token_s, x_s.at[own_slot, :, :, lanes], tok_s.at[n], tok_r.at[n], (peer(n), b))
        )
    for copy in gathers:
        copy.start()
    x_s[own_slot, :, :, lanes] = token_s[...]
    to_mate = [remote(token_s, x_s.at[own_mate_slot, :, :, lanes], mate_s.at[0], mate_r.at[0], mate)]
    to_mate[0].start()
    for n in ORDER:
        here, there = slots(source(n))
        remote(
            token_s, x_s.at[here, :, :, lanes], tok_s.at[n], tok_r.at[n], (peer(n), b)
        ).wait_recv()
        copy = remote(
            x_s.at[here, :, :, lanes], x_s.at[there, :, :, lanes], mate_s.at[n], mate_r.at[n], mate
        )
        copy.start()
        to_mate.append(copy)
    for load in loads[:2]:
        load.wait()
    for push in pushes[:3]:
        push.wait()
    for copy in to_mate:
        copy.wait_recv()
    pushes[3].start()

    lane = lax.broadcasted_iota(jnp.int32, (32, 128), 1)

    def project(s):
        tokens = x_s[pl.ds(s * 2, 2)].reshape(128, 2 * FEAT)
        return tokens

    def up_pair(s):
        tokens = project(s)
        for lo in range(0, HALF, 512):
            hi = min(lo + 512, HALF)
            part = jnp.dot(tokens, up_w[:, lo:hi], preferred_element_type=F32)
            pu[pl.ds(s * 2, 2), :, :, lo:hi] = part.reshape(2, 2, 32, hi - lo)
        plain = [
            tokens[:, c * FEAT : (c + 1) * FEAT].astype(F32) * inv_gain[c, 0:1] for c in range(2)
        ]
        squares = plain[0] * plain[0] + plain[1] * plain[1]
        total = jnp.sum(squares, axis=1, keepdims=True)
        pu[pl.ds(s * 2, 2), :, :, HALF:] = jnp.broadcast_to(total, (128, 128)).reshape(2, 2, 32, 128)

    def gate_pair(s):
        tokens = project(s)
        for lo in range(0, HALF, 512):
            hi = min(lo + 512, HALF)
            part = jnp.dot(tokens, gate_w[:, lo:hi], preferred_element_type=F32)
            pg[pl.ds(s * 2, 2), :, :, lo:hi] = part.reshape(2, 2, 32, hi - lo)
        xg_send[pl.ds(s * 2, 2)] = pg[pl.ds(s * 2, 2), x_other].astype(BF16)

    def xg_copy(s):
        two = pl.ds(s * 2, 2)
        return remote(xg_send.at[two], xg_recv.at[two], xg_ss.at[s], xg_rs.at[s], xmate)

    def up_sum(block, half, arrived):
        body = pu[block, half, :, :HALF]
        squares = pu[block, half, :, HALF:]
        for ref in arrived:
            body = body + ref[:, :HALF].astype(F32)
            halves = ref[:, HALF:].astype(F32)
            squares = squares + halves + pltpu.roll(halves, 64, 1)
        return body, squares

    def put_up(ref, body, squares):
        ref[:, :HALF] = body.astype(BF16)
        high = squares.astype(BF16)
        low = (squares - high.astype(F32)).astype(BF16)
        ref[:, HALF:] = jnp.where(lane < 64, high.astype(F32), low.astype(F32)).astype(BF16)

    halves = (x_other, x)
    sent = []

    def ua_copy(s, n):
        h = halves[n]
        return remote(ua_send.at[s, h], ua_recv.at[s, h], ua_ss.at[s, n], ua_rs.at[s, n], ahead)

    def ub_copy(s, n):
        h = halves[n]
        return remote(ub_send.at[s, h], ub_recv.at[s, h], ub_ss.at[s, n], ub_rs.at[s, n], behind)

    def ga_copy(s):
        return remote(ga_send.at[s], ga_recv.at[s], ga_ss.at[s], ga_rs.at[s], ahead)

    def gb_copy(s):
        return remote(gb_send.at[s], gb_recv.at[s], gb_ss.at[s], gb_rs.at[s], behind)

    def up_step(s):
        for n in range(2):
            h = halves[n]
            if s > 0:
                ua_copy(s - 1, n).wait_recv()
            arrived = [ua_recv.at[s - 1, h]] if s > 0 else []
            put_up(ua_send.at[s, h], *up_sum(2 * s, h, arrived))
            ua_copy(s, n).start()
            sent.append(ua_copy(s, n))
            if s < 3:
                if s > 0:
                    ub_copy(s - 1, n).wait_recv()
                arrived = [ub_recv.at[s - 1, h]] if s > 0 else []
                put_up(ub_send.at[s, h], *up_sum(2 * s + 1, h, arrived))
                ub_copy(s, n).start()
                sent.append(ub_copy(s, n))

    def gate_step(s):
        xg_copy(s).wait_recv()
        if s > 0:
            ga_copy(s - 1).wait_recv()
        total = pg[2 * s, x] + xg_recv[2 * s].astype(F32)
        if s > 0:
            total = total + ga_recv[s - 1].astype(F32)
        ga_send[s] = total.astype(BF16)
        ga_copy(s).start()
        sent.append(ga_copy(s))
        if s < 3:
            if s > 0:
                gb_copy(s - 1).wait_recv()
            total = pg[2 * s + 1, x] + xg_recv[2 * s + 1].astype(F32)
            if s > 0:
                total = total + gb_recv[s - 1].astype(F32)
            gb_send[s] = total.astype(BF16)
            gb_copy(s).start()
            sent.append(gb_copy(s))

    up_pair(0)
    up_step(0)
    gate_pair(0)
    xg_copy(0).start()

    def pairs(s, carry):
        gate_pair(s)
        xg_copy(s).start()
        up_pair(s)
        return carry

    lax.fori_loop(1, 4, pairs, 0)
    gate_step(0)
    for s in range(1, 4):
        up_step(s)
        gate_step(s)

    xu_copy = remote(xu_send, xu_recv, xu_ss, xu_rs, xmate)
    for n in range(2):
        ua_copy(3, n).wait_recv()
        ub_copy(2, n).wait_recv()
        h = halves[n]
        body, squares = up_sum(7, h, [ua_recv.at[3, h], ub_recv.at[2, h]])
        if n == 0:
            put_up(xu_send, body, squares)
            xu_copy.start()
        else:
            pu[7, h, :, :HALF] = body
            pu[7, h, :, HALF:] = squares
    ga_copy(3).wait_recv()
    gb_copy(2).wait_recv()
    gate_sum = pg[7, x] + xg_recv[7].astype(F32) + ga_recv[3].astype(F32) + gb_recv[2].astype(F32)
    xu_copy.wait_recv()
    up_total, squares = up_sum(7, x, [xu_recv])
    scale = lax.rsqrt(squares[:, 0:1] / D + 1e-05)
    gate_sum = gate_sum * scale
    hidden = (gate_sum / (1.0 + jnp.exp(-gate_sum)) * (up_total * scale)).astype(BF16)
    h1[0, x] = hidden[:, :C1]
    h2[0, x] = hidden[:, C1:]

    def hidden_ref(kind, pos):
        return (h1.at[pos, x], h1.at[pos, x_other], h2.at[pos, x])[kind]

    def hz_copy(kind, pos, target, to):
        return remote(
            hidden_ref(kind, pos), hidden_ref(kind, target), hz_s.at[kind, target], hz_r.at[kind, target], to
        )

    def hx_copy(n, ref):
        return remote(ref, ref, hx_s.at[n], hx_r.at[n], xmate)

    def forward(kind, pos):
        if pos == 0:
            targets = ((1, ahead), (2, behind))
        elif pos % 2 == 1:
            targets = ((pos + 2, ahead),) if pos < 7 else ()
        else:
            targets = ((pos + 2, behind),) if pos < 6 else ()
        for target, to in targets:
            copy = hz_copy(kind, pos, target, to)
            copy.start()
            sent.append(copy)

    def to_xmate(pos):
        copy = hx_copy(pos, h2.at[pos, x])
        copy.start()
        sent.append(copy)

    def down_step(k):
        first, count = (0, 1) if k == 0 else (2 * k - 1, 2 if k < 4 else 1)
        for pos in range(first, first + count):
            hx_copy(pos, h2.at[pos, x_other]).wait_recv()
        left = h1[first : first + count].reshape(count * 64, C1)
        right = h2[first : first + count].reshape(count * 64, C2)
        for c in range(2):
            dp[k, c, : count * 64] = jnp.dot(
                left, down_w[c, :C1], preferred_element_type=F32
            ) + jnp.dot(right, down_w[c, C1:], preferred_element_type=F32)
        some = pl.ds(0, count * 64)
        copy = remote(
            dp.at[k, 1 - core, some], dr.at[k, some], dr_s.at[k], dr_r.at[k], mate
        )
        copy.start()
        sent.append(copy)

    def return_copy(pos, owner):
        return remote(ds_send.at[pos], fr.at[g], fr_s.at[pos], fr_r.at[g], (owner, b))

    returns = []

    def return_step(k):
        first, count = (0, 1) if k == 0 else (2 * k - 1, 2 if k < 4 else 1)
        some = pl.ds(0, count * 64)
        remote(dp.at[k, 1 - core, some], dr.at[k, some], dr_s.at[k], dr_r.at[k], mate).wait_recv()
        for j in range(count):
            pos = first + j
            there = count - 1 - j
            total = (
                dp[k, core, j * 64 : j * 64 + 64] + dr[k, there * 64 : there * 64 + 64]
            ).astype(BF16)
            ds_send[pos] = total
            owner = lax.rem(z + (-sign if j == 0 else sign) * k + RING, RING)
            returns.append((pos, owner))

            @pl.when(owner != g)
            def _():
                return_copy(pos, owner).start()

            @pl.when(owner == g)
            def _():
                fr[g] = total

    forward(2, 0)
    forward(0, 0)
    copy = hx_copy(8, h1.at[0, x])
    copy.start()
    sent.append(copy)
    to_xmate(0)
    pushes[3].wait()
    loads[2].wait()
    hx_copy(8, h1.at[0, x_other]).wait_recv()
    forward(1, 0)
    for k in range(1, 5):
        for kind in (2, 0, 1):
            for pos in (2 * k - 1, 2 * k) if k < 4 else (7,):
                hz_copy(kind, pos, pos, ahead).wait_recv()
                forward(kind, pos)
                if kind == 2:
                    to_xmate(pos)
        if k >= 2:
            return_step(k - 2)
        down_step(k - 1)
    return_step(3)
    down_step(4)
    return_step(4)

    total = wide_s[...]
    for n in ORDER:
        remote(
            ds_send.at[0], fr.at[source(n)], fr_s.at[0], fr_r.at[source(n)], (peer(n), b)
        ).wait_recv()
    for j in range(GROUPS):
        total = total + fr[j].astype(F32)
    out[...] = total

    for copy in merges + gathers + to_mate:
        copy.wait_send()
    for s in range(4):
        xg_copy(s).wait_send()
    xu_copy.wait_send()
    for copy in sent:
        copy.wait_send()
    for pos, owner in returns:

        @pl.when(owner != g)
        def _():
            return_copy(pos, owner).wait_send()


def feed_forward(w_in, st_in, res, gain, gate, up, down):
    vmem = pl.BlockSpec(memory_space=pltpu.VMEM)
    hbm = pl.BlockSpec(memory_space=pl.ANY)
    V = pltpu.VMEM
    dma = lambda *shape: pltpu.SemaphoreType.DMA(shape)
    scratch = [
        V((4, 64, FEAT), BF16), V((4, 64, 128), F32), V((64, FEAT), F32), V((2, 32, FEAT), BF16),
        V((2, 8, FEAT), F32),
        V((2 * FEAT, HALF), BF16), V((2 * FEAT, HALF), BF16), V((2, HALF, FEAT), BF16),
        V((8, 2, 32, 2 * FEAT), BF16), V((8, 2, 32, WIDE), F32), V((8, 2, 32, HALF), F32),
        V((8, 32, HALF), BF16), V((8, 32, HALF), BF16),
        V((4, 2, 32, WIDE), BF16), V((4, 2, 32, WIDE), BF16),
        V((3, 2, 32, WIDE), BF16), V((3, 2, 32, WIDE), BF16),
        V((4, 32, HALF), BF16), V((4, 32, HALF), BF16),
        V((3, 32, HALF), BF16), V((3, 32, HALF), BF16),
        V((32, WIDE), BF16), V((32, WIDE), BF16),
        V((8, 2, 32, C1), BF16), V((8, 2, 32, C2), BF16),
        V((5, 2, 128, FEAT), F32), V((5, 128, FEAT), F32),
        V((8, 64, FEAT), BF16), V((8, 64, FEAT), BF16),
        dma(3), dma(4), dma(4), dma(8), dma(8), dma(8), dma(8), dma(8), dma(8),
        dma(4), dma(4), dma(4, 2), dma(4, 2), dma(3, 2), dma(3, 2),
        dma(4), dma(4), dma(3), dma(3), pltpu.SemaphoreType.DMA, pltpu.SemaphoreType.DMA,
        dma(3, 8), dma(3, 8), dma(9), dma(9), dma(5), dma(5), dma(8), dma(8),
    ]
    return pl.pallas_call(
        kernel,
        out_shape=jax.ShapeDtypeStruct((64, FEAT), F32),
        in_specs=[vmem, vmem, vmem, vmem, hbm, hbm, hbm],
        out_specs=vmem,
        scratch_shapes=scratch,
        compiler_params=pltpu.CompilerParams(
            collective_id=0, has_side_effects=True, vmem_limit_bytes=50 * 1024 * 1024
        ),
        cost_estimate=pl.CostEstimate(
            flops=5_300_000_000, bytes_accessed=11_000_000, transcendentals=100_000
        ),
    )(w_in, st_in, res, gain, gate, up, down)


def on_device(
    residual_in,
    queries,
    key_cache,
    value_cache,
    key_new,
    value_new,
    lengths,
    ffn_gain,
    gate_weight,
    up_weight,
    down_weight,
):
    cycle_size = lax.axis_size("blk")
    quarters = cycle_size // KV_HEADS
    per_kv = HEADS // KV_HEADS
    own_heads = HEADS // cycle_size
    head_size = key_cache.shape[3]
    seq_rows = residual_in.shape[0]
    positions_here = key_cache.shape[2]
    blk_index = lax.axis_index("blk")
    kv_head = blk_index // quarters
    quarter = blk_index % quarters
    score_scale = 1.0 / math.sqrt(head_size)
    group_queries = lax.dynamic_slice_in_dim(
        queries, kv_head * per_kv * head_size, per_kv * head_size, 1
    )
    group_queries = group_queries.astype(F32).reshape(seq_rows, per_kv, head_size)
    fresh_key = lax.dynamic_slice_in_dim(key_new, kv_head * head_size, head_size, 1).astype(F32)
    fresh_value = lax.dynamic_slice_in_dim(value_new, kv_head * head_size, head_size, 1).astype(F32)
    keys_here = key_cache[:, 0].astype(F32)
    values_here = value_cache[:, 0].astype(F32)
    scores = jnp.einsum("shd,spd->shp", group_queries, keys_here) * score_scale
    fresh_scores = jnp.einsum("shd,sd->sh", group_queries, fresh_key) * score_scale
    places = quarter * positions_here + jnp.arange(positions_here, dtype=jnp.int32)
    usable = (places[None, :] < lengths[:, None])[:, None, :]
    with_fresh = quarter == 0
    largest = jnp.maximum(
        jnp.max(jnp.where(usable, scores, -1e30), axis=2),
        jnp.where(with_fresh, fresh_scores, -1e30),
    )
    weights = jnp.where(usable, jnp.exp(scores - largest[..., None]), 0.0)
    fresh_weight = jnp.where(with_fresh, jnp.exp(fresh_scores - largest), 0.0)
    totals = jnp.sum(weights, axis=2) + fresh_weight
    weighted = (
        jnp.einsum("shp,spd->shd", weights, values_here)
        + fresh_weight[..., None] * fresh_value[:, None, :]
    )
    w_in = weighted.astype(BF16).reshape(seq_rows, quarters, own_heads * head_size).transpose(1, 0, 2)
    stats = jnp.concatenate(
        [largest.reshape(seq_rows, quarters, own_heads), totals.reshape(seq_rows, quarters, own_heads)],
        axis=2,
    )
    st_in = jnp.pad(stats, ((0, 0), (0, 0), (0, 128 - 2 * own_heads))).transpose(1, 0, 2)
    return feed_forward(
        w_in, st_in, residual_in, ffn_gain.reshape(1, FEAT), gate_weight, up_weight, down_weight
    )


def solution(mesh):
    in_specs = (
        P("grp", "blk"),
        P("grp", None),
        P("grp", "blk", None, None),
        P("grp", "blk", None, None),
        P("grp", None),
        P("grp", None),
        P("grp"),
        P("blk"),
        P("blk", "grp"),
        P("blk", "grp"),
        P("grp", "blk"),
    )
    out_specs = P("grp", "blk")
    return jax.shard_map(
        on_device, mesh=mesh, in_specs=in_specs, out_specs=out_specs, check_vma=False
    )
```

time: 557 us -> 96.9 us (0.17)
  waiting for transfers between devices: 413 us -> 0 us
  Pallas kernels: 0 us -> 85.6 us
  blocking collectives: 81.7 us -> 0 us
  matrix products: 22.1 us -> 3.92 us
  other arithmetic: 18.7 us -> 2.03 us
  between operations: 13.5 us -> 0.17 us
    psum x1 -> x0, waiting for transfers between devices: 322 us -> none  [on_device(): summed = lax.psum(partial_sums, 'blk')]
    pallas_call x0 -> x1, Pallas kernels: none -> 85.6 us  [feed_forward(): pl.pallas_call(kernel, out_shape=jax.ShapeDtypeStruct((64, FEAT), F32), i...]
    reduce_scatter x1 -> x0, waiting for transfers between devices: 76.2 us -> none  [on_device(): lax.psum_scatter(down_terms, 'grp', scatter_dimension=0, tiled=True)]
    psum x1 -> x0, blocking collectives: 52.6 us -> none  [on_device(): row_total = lax.psum(jnp.sum(wide * wide, axis=1), 'blk')]
    all_gather x1 -> x0, blocking collectives: 29.1 us -> none  [on_device(): piece = lax.all_gather(normed, 'grp', axis=0, tiled=True)]
    dot_general x3 -> x0, matrix products: 18.2 us -> none  [the longest x1 8.75 us: on_device(): jnp.dot(hidden, down_weight, preferred_element_type=jnp.float32)]
    ppermute x6 -> x0, waiting for transfers between devices: 13.9 us -> none  [partner(): lax.ppermute(x, axis, [(i, i ^ 1 << distance) for i in range(lax.axis_siz...]
    another operation x1 -> x0, other arithmetic: 10.6 us -> none  [on_device(): partial_sums = jnp.stack([gate_part, up_part], axis=1)]
  transfers between devices with their start and end apart: 8 -> 0, of which waited for: 5 -> 0; matrix products, arithmetic and copies ran while one was open for 0% -> 0% of each run, Pallas kernels for 0% -> 0%
where the time goes in v1:
time: 96.9 us; the launch traced here: 96.2 us
  Pallas kernels  85.6 us (88%)
  local copies, waits for them, and re-layouts  4.49 us (5%)
  matrix products  3.92 us (4%)
  other arithmetic  2.03 us (2%)
    pallas_call x1, Pallas kernels, feed_forward(): pl.pallas_call(kernel, out_shape=jax.ShapeDtypeStruct((64, FEAT), F32), i...  85.6 us
    unnamed x11, local copies, waits for them, and re-layouts  3.38 us
    dot_general x1, matrix products, on_device(): scores = jnp.einsum('shd,spd->shp', group_queries, keys_here) * score_scale  1.99 us

profile of v1, /device:TPU:7, one launch (start us, length us, event | category | flops | bytes accessed | tf_op | source)
XLA Modules:
  0.0 96.2 jit_solution(6444051861304880068)
XLA Ops:
  0.0 0.0 copy-start
  0.0 0.9 broadcast_compare_fusion
  0.9 0.7 copy-done
  1.7 0.0 copy-start.3
  1.7 0.0 copy-start.2
  1.7 2.0 %select_reduce_fusion = (f32[64,16]{1,0:T(8,128)S(1)}, f32[64,16,64]{2,1,0:T(8,128)S(1)}) fusion(pred[64,64]{1,0:T(8,128)(4,1)S(1)} %broadcast_compare_fusion, bf16[64,16,128]{2,1,0:T(8,128)(2,1)S(1)} %bitcast.25, bf16[64,1,64,128]{3,2,1,0:T(8,128)(2,1)} %param.13), kind=kOutput, calls=%fused_computation.6 | convolution fusion | flops 16972800 | bytes 1581056 | tf_op jit(solution)/shard_map/shd,spd->shp/dot_general | solution.py:490
  3.7 0.7 dynamic-slice_convert_fusion
  4.4 0.7 dynamic-slice_bitcast_fusion.1
  5.1 0.2 fusion.7
  5.4 0.4 fusion.3
  5.8 1.7 %fusion = bf16[64,16,128]{2,1,0:T(8,128)(2,1)S(1)} fusion(bf16[64,1,64,128]{3,2,1,0:T(8,128)(2,1)} %param.14, f32[64,16,64]{2,1,0:T(8,128)S(1)} %get-tuple-element.8, f32[64,128]{1,0:T(8,128)S(1)} %dynamic-slice_convert_fusion, f32[64,16]{1,0:T(8,128)S(1)} %get-tuple-element.6, f32[64,16]{1,0:T(8,128)S(1)} %select_maximum_fusion, ...), kind=kOutput, calls=%fused_computation.2 | convolution fusion | flops 17301504 | bytes 1617920 | tf_op jit(solution)/shard_map/shp,spd->shd/dot_general | solution.py:503
  7.5 0.1 reshape.46
  7.7 0.1 copy.19
  7.7 0.1 copy.18
  7.8 0.1 copy.20
  7.9 0.0 copy-done.3
  8.0 0.0 copy-done.2
  8.0 0.0 copy-start.1
  8.0 2.0 %copy-done.1 = bf16[512,3328]{1,0:T(8,128)(2,1)S(1)} copy-done((bf16[512,3328]{1,0:T(8,128)(2,1)S(1)}, bf16[512,3328]{1,0:T(8,128)(2,1)}, u32[]{:S(2)}) %copy-start.1) | copy-done | bytes 3407896
  9.9 85.6 %shard_map.109 = f32[64,512]{1,0:T(8,128)S(1)} custom-call(bf16[4,64,512]{2,1,0:T(8,128)(2,1)S(1)} %bitcast.24, f32[4,64,128]{2,1,0:T(8,128)S(1)} %pad_bitcast_fusion.st_in, bf16[64,512]{1,0:T(8,128)(2,1)S(1)} %copy-done.2, bf16[1,512]{1,0:T(2,128)(2,1)S(1)} %reshape.49.gain, bf16[512,3328]{1,0:T(8,128)(2,1)S(1)} %copy-done.1, bf16[512,3328]{1,0:T(8,128)(2,1)} %up.1, ...), custom_call_target="tpu_custom_call" | custom-call | flops 5299999744 | bytes 11000000 | tf_op jit(solution)/shard_map/pallas_call | solution.py:443
  95.5 0.7 copy.29
  (9 shorter events, 0.2 us)
Async XLA Ops:
  0.0 1.6 %copy-start = (bf16[64,16384]{1,0:T(8,128)(2,1)S(1)}, bf16[64,16384]{1,0:T(8,128)(2,1)}, u32[]{:S(2)}) copy-start(bf16[64,16384]{1,0:T(8,128)(2,1)} %param.12) | copy-start | bytes 6291460
  1.7 6.3 %copy-start.3 = (bf16[512]{0:T(512)(128)(2,1)S(1)}, bf16[512]{0:T(512)(128)(2,1)}, u32[]{:S(2)}) copy-start(bf16[512]{0:T(512)(128)(2,1)} %param.18) | copy-start | bytes 3076
  1.7 6.3 %copy-start.2 = (bf16[64,512]{1,0:T(8,128)(2,1)S(1)}, bf16[64,512]{1,0:T(8,128)(2,1)}, u32[]{:S(2)}) copy-start(bf16[64,512]{1,0:T(8,128)(2,1)} %res.1) | copy-start | bytes 196612
  8.0 2.0 %copy-start.1 = (bf16[512,3328]{1,0:T(8,128)(2,1)S(1)}, bf16[512,3328]{1,0:T(8,128)(2,1)}, u32[]{:S(2)}) copy-start(bf16[512,3328]{1,0:T(8,128)(2,1)} %gate.1) | copy-start | bytes 10223620

commit v2 on v1

--- a/solution.py
+++ b/solution.py
@@ -29,13 +29,13 @@
 
 
 def kernel(
-    w_in, st_in, res, gain, gate, up, down, out,
-    w_got, st_got, wide_s, token_s, inv_gain,
+    queries, keys, values, key_new, value_new, lengths, res_in, gain_in, gate, up, down, out,
+    q_s, k_s, v_s, kn_s, vn_s, len_s, res, gain, q32, kn32, vn32, att, stats_s, w_in, st_in, w_got, st_got, wide_s, token_s, inv_gain,
     gate_w, up_w, down_w, x_s, pu, pg,
     xg_send, xg_recv, ua_send, ua_recv, ub_send, ub_recv,
     ga_send, ga_recv, gb_send, gb_recv, xu_send, xu_recv,
     h1, h2, dp, dr, ds_send, fr,
-    local_sem, wsem_s, wsem_r, at_s, at_r, tok_s, tok_r, mate_s, mate_r,
+    load_sem, local_sem, wsem_s, wsem_r, at_s, at_r, tok_s, tok_r, mate_s, mate_r,
     xg_ss, xg_rs, ua_ss, ua_rs, ub_ss, ub_rs, ga_ss, ga_rs, gb_ss, gb_rs, xu_ss, xu_rs,
     hz_s, hz_r, hx_s, hx_r, dr_s, dr_r, fr_s, fr_r,
 ):
@@ -68,57 +68,128 @@
     mine = pl.ds(pl.multiple_of(core * HALF, 128), HALF)
     other = pl.ds(pl.multiple_of((1 - core) * HALF, 128), HALF)
     rows = pl.ds(pl.multiple_of(core * FEAT, FEAT), FEAT)
+    head_lanes = pl.ds(pl.multiple_of(z * 128, 128), 128)
+    cache_loads = [
+        pltpu.make_async_copy(
+            queries.at[:, pl.ds(pl.multiple_of(z * 2048, 2048), 2048)], q_s, load_sem.at[0]
+        ),
+        pltpu.make_async_copy(key_new.at[:, head_lanes], kn_s, load_sem.at[1]),
+        pltpu.make_async_copy(value_new.at[:, head_lanes], vn_s, load_sem.at[2]),
+        pltpu.make_async_copy(lengths, len_s, load_sem.at[5]),
+        pltpu.make_async_copy(keys.at[:, 0], k_s, load_sem.at[3]),
+        pltpu.make_async_copy(values.at[:, 0], v_s, load_sem.at[4]),
+        pltpu.make_async_copy(res_in, res, load_sem.at[6]),
+        pltpu.make_async_copy(gain_in, gain, load_sem.at[7]),
+    ]
+    for load in cache_loads:
+        load.start()
     loads = [
         pltpu.make_async_copy(gate.at[:, mine], gate_w.at[rows], local_sem.at[0]),
         pltpu.make_async_copy(up.at[:, mine], up_w.at[rows], local_sem.at[1]),
         pltpu.make_async_copy(down.at[mine], down_w.at[core], local_sem.at[2]),
     ]
-    for load in loads:
-        load.start()
-
+    st_got[...] = jnp.zeros((128, 128), F32)
     barrier = pltpu.get_barrier_semaphore()
     partners = [mate, xmate, (g, z * 4 + (1 - x) * 2 + (1 - core)), ahead, behind]
     partners += [(peer(n), b) for n in ORDER]
     for partner in partners:
         pl.semaphore_signal(barrier, inc=1, device_id=partner, device_id_type=MESH)
 
-    inv_gain[core] = jnp.broadcast_to(1.0 / gain[...].astype(F32), (8, FEAT))
     pl.semaphore_wait(barrier, len(partners))
 
-    merges = []
-    for n in (3, 2, 1):
-        p = q ^ n
-        to = (g, z * 4 + p)
-        merges.append(remote(st_in.at[p], st_got.at[q], at_s.at[n], at_r.at[q], to))
-        merges.append(remote(w_in.at[p], w_got.at[q], at_s.at[4 + n], at_r.at[4 + q], to))
-    for copy in merges:
-        copy.start()
     pushes = [
         remote(inv_gain.at[core], inv_gain.at[core], wsem_s.at[0], wsem_r.at[0], mate),
         remote(up.at[:, other], up_w.at[rows], wsem_s.at[1], wsem_r.at[1], mate),
         remote(gate.at[:, other], gate_w.at[rows], wsem_s.at[2], wsem_r.at[2], mate),
         remote(down.at[other], down_w.at[core], wsem_s.at[3], wsem_r.at[3], mate),
     ]
+    for load in cache_loads:
+        load.wait()
+    for load in loads[:2]:
+        load.start()
+    gain_row = gain[...].astype(F32).reshape(1, FEAT)
+    inv_gain[core] = jnp.broadcast_to(1.0 / gain_row, (8, FEAT))
     for push in pushes[:3]:
         push.start()
-    st_got[q] = st_in[q]
+    loads[2].start()
+    q32[...] = q_s[...].astype(F32)
+    kn32[...] = kn_s[...].astype(F32)
+    vn32[...] = vn_s[...].astype(F32)
+    score_scale = 1.0 / math.sqrt(128)
+    lane8 = lax.broadcasted_iota(jnp.int32, (8, 128), 1)
+    row8 = lax.broadcasted_iota(jnp.int32, (8, 128), 0)
+    row = lax.broadcasted_iota(jnp.int32, (128, 512), 0)
+    col = lax.broadcasted_iota(jnp.int32, (128, 512), 1)
+    same = lax.rem(row, 8) == col // 64
+    place = q * 64 + lax.rem(col, 64)
+
+    def attend(i, carry):
+        eight = pl.ds(pl.multiple_of(i * 8, 8), 8)
+        q8 = q32[eight]
+        q_rows = jnp.concatenate([q8[:, h * 128 : h * 128 + 128] for h in range(16)], axis=0)
+        k_rows = k_s[eight].reshape(512, 128)
+        v_rows = v_s[eight].reshape(512, 128)
+        spread = lambda a: jnp.concatenate([a] * 16, axis=0)
+        limit = jnp.zeros((8, 128), jnp.int32)
+        for n in range(8):
+            limit = jnp.where(row8 == n, len_s[i * 8 + n], limit)
+        usable = same & (place < spread(limit)[:, 0:1])
+        scores = lax.dot_general(
+            q_rows.astype(BF16), k_rows, (((1,), (1,)), ((), ())), preferred_element_type=F32
+        )
+        scores = jnp.where(usable, scores * score_scale, -1e30)
+        fresh = jnp.sum(q_rows * spread(kn32[eight]), axis=1, keepdims=True) * score_scale
+        fresh = jnp.where(q == 0, fresh, -1e30)
+        top = jnp.maximum(jnp.max(scores, axis=1, keepdims=True), fresh)
+        weights = jnp.where(usable, jnp.exp(scores - top), 0.0)
+        fresh_weight = jnp.where(q == 0, jnp.exp(fresh - top), 0.0)
+        total = jnp.sum(weights, axis=1, keepdims=True) + fresh_weight
+        mixed = jnp.dot(weights.astype(BF16), v_rows, preferred_element_type=F32)
+        mixed = mixed + fresh_weight * spread(vn32[eight])
+        att[:, eight] = mixed.reshape(16, 8, 128)
+        stats = jnp.zeros((8, 128), F32)
+        for h in range(16):
+            at = h // 4 * 8 + h % 4
+            stats = jnp.where(lane8 == at, top[h * 8 : h * 8 + 8], stats)
+            stats = jnp.where(lane8 == at + 4, total[h * 8 : h * 8 + 8], stats)
+        stats_s[eight] = stats
+        return carry
+
+    stats_s[64:] = jnp.zeros((64, 128), F32)
+    lax.fori_loop(0, 8, attend, 0, unroll=8)
+    st_in[...] = jnp.transpose(stats_s[...])[:32]
+    w_in[...] = att[...].astype(BF16).reshape(4, 4, 64, 128)
+
+    eight_of = lambda n: pl.ds(pl.multiple_of(n * 8, 8), 8)
+    merges = []
+    for n in (3, 2, 1):
+        p = q ^ n
+        to = (g, z * 4 + p)
+        merges.append(remote(st_in.at[eight_of(p)], st_got.at[eight_of(q)], at_s.at[n], at_r.at[q], to))
+        merges.append(remote(w_in.at[p], w_got.at[q], at_s.at[4 + n], at_r.at[4 + q], to))
+    for copy in merges:
+        copy.start()
+    st_got[eight_of(q)] = st_in[eight_of(q)]
     w_got[q] = w_in[q]
     for n in (1, 2, 3):
         p = q ^ n
         to = (g, z * 4 + p)
-        remote(st_in.at[p], st_got.at[p], at_s.at[n], at_r.at[p], to).wait_recv()
+        remote(
+            st_in.at[eight_of(p)], st_got.at[eight_of(p)], at_s.at[n], at_r.at[p], to
+        ).wait_recv()
         remote(w_in.at[p], w_got.at[p], at_s.at[4 + n], at_r.at[4 + p], to).wait_recv()
+    got = jnp.transpose(st_got[...])[:64]
     for head in range(4):
         cols = slice(head * 128, head * 128 + 128)
-        tops = [st_got[j][:, head : head + 1] for j in range(4)]
-        sums = [st_got[j][:, 4 + head : 5 + head] for j in range(4)]
+        tops = [got[:, j * 8 + head : j * 8 + head + 1] for j in range(4)]
+        sums = [got[:, j * 8 + head + 4 : j * 8 + head + 5] for j in range(4)]
         top = jnp.maximum(jnp.maximum(tops[0], tops[1]), jnp.maximum(tops[2], tops[3]))
         factors = [jnp.exp(t - top) for t in tops]
         total = sum(f * s for f, s in zip(factors, sums))
-        mixed = sum(f * w_got[j, :, cols].astype(F32) for j, f in enumerate(factors))
+        mixed = sum(f * w_got[j, head].astype(F32) for j, f in enumerate(factors))
         wide = res[:, cols].astype(F32) + mixed / total
         wide_s[:, cols] = wide
-        scaled = (wide * gain[:, cols].astype(F32)).astype(BF16)
+        scaled = (wide * gain_row[:, cols]).astype(BF16)
         token_s[0, :, cols] = scaled[:32]
         token_s[1, :, cols] = scaled[32:]
 
@@ -153,9 +224,22 @@
         load.wait()
     for push in pushes[:3]:
         push.wait()
+
+    other_rows = pl.ds(pl.multiple_of((1 - core) * FEAT, FEAT), FEAT)
+
+    def up_first(lanes_of, add):
+        tokens = x_s[pl.ds(0, 2), :, :, lanes_of].reshape(128, FEAT)
+        for lo in range(0, HALF, 512):
+            hi = min(lo + 512, HALF)
+            part = jnp.dot(tokens, up_w[lanes_of, lo:hi], preferred_element_type=F32)
+            part = part.reshape(2, 2, 32, hi - lo)
+            pu[0:2, :, :, lo:hi] = pu[0:2, :, :, lo:hi] + part if add else part
+
+    up_first(rows, False)
     for copy in to_mate:
         copy.wait_recv()
     pushes[3].start()
+    up_first(other_rows, True)
 
     lane = lax.broadcasted_iota(jnp.int32, (32, 128), 1)
 
@@ -169,6 +253,10 @@
             hi = min(lo + 512, HALF)
             part = jnp.dot(tokens, up_w[:, lo:hi], preferred_element_type=F32)
             pu[pl.ds(s * 2, 2), :, :, lo:hi] = part.reshape(2, 2, 32, hi - lo)
+        square_sums(s)
+
+    def square_sums(s):
+        tokens = project(s)
         plain = [
             tokens[:, c * FEAT : (c + 1) * FEAT].astype(F32) * inv_gain[c, 0:1] for c in range(2)
         ]
@@ -184,9 +272,8 @@
             pg[pl.ds(s * 2, 2), :, :, lo:hi] = part.reshape(2, 2, 32, hi - lo)
         xg_send[pl.ds(s * 2, 2)] = pg[pl.ds(s * 2, 2), x_other].astype(BF16)
 
-    def xg_copy(s):
-        two = pl.ds(s * 2, 2)
-        return remote(xg_send.at[two], xg_recv.at[two], xg_ss.at[s], xg_rs.at[s], xmate)
+    def xg_copy(n):
+        return remote(xg_send.at[n], xg_recv.at[n], xg_ss.at[n], xg_rs.at[n], xmate)
 
     def up_sum(block, half, arrived):
         body = pu[block, half, :, :HALF]
@@ -238,7 +325,7 @@
                 sent.append(ub_copy(s, n))
 
     def gate_step(s):
-        xg_copy(s).wait_recv()
+        xg_copy(2 * s).wait_recv()
         if s > 0:
             ga_copy(s - 1).wait_recv()
         total = pg[2 * s, x] + xg_recv[2 * s].astype(F32)
@@ -248,6 +335,7 @@
         ga_copy(s).start()
         sent.append(ga_copy(s))
         if s < 3:
+            xg_copy(2 * s + 1).wait_recv()
             if s > 0:
                 gb_copy(s - 1).wait_recv()
             total = pg[2 * s + 1, x] + xg_recv[2 * s + 1].astype(F32)
@@ -257,14 +345,16 @@
             gb_copy(s).start()
             sent.append(gb_copy(s))
 
-    up_pair(0)
+    square_sums(0)
     up_step(0)
     gate_pair(0)
     xg_copy(0).start()
+    xg_copy(1).start()
 
     def pairs(s, carry):
         gate_pair(s)
-        xg_copy(s).start()
+        xg_copy(2 * s).start()
+        xg_copy(2 * s + 1).start()
         up_pair(s)
         return carry
 
@@ -286,6 +376,7 @@
         else:
             pu[7, h, :, :HALF] = body
             pu[7, h, :, HALF:] = squares
+    xg_copy(7).wait_recv()
     ga_copy(3).wait_recv()
     gb_copy(2).wait_recv()
     gate_sum = pg[7, x] + xg_recv[7].astype(F32) + ga_recv[3].astype(F32) + gb_recv[2].astype(F32)
@@ -325,33 +416,43 @@
         copy.start()
         sent.append(copy)
 
-    def down_step(k):
-        first, count = (0, 1) if k == 0 else (2 * k - 1, 2 if k < 4 else 1)
-        for pos in range(first, first + count):
-            hx_copy(pos, h2.at[pos, x_other]).wait_recv()
-        left = h1[first : first + count].reshape(count * 64, C1)
-        right = h2[first : first + count].reshape(count * 64, C2)
-        for c in range(2):
-            dp[k, c, : count * 64] = jnp.dot(
-                left, down_w[c, :C1], preferred_element_type=F32
-            ) + jnp.dot(right, down_w[c, C1:], preferred_element_type=F32)
-        some = pl.ds(0, count * 64)
-        copy = remote(
-            dp.at[k, 1 - core, some], dr.at[k, some], dr_s.at[k], dr_r.at[k], mate
-        )
-        copy.start()
-        sent.append(copy)
+    def step_blocks(k):
+        return (0, 1) if k == 0 else (2 * k - 1, 2 if k < 4 else 1)
+
+    def mate_sums(k):
+        some = pl.ds(0, step_blocks(k)[1] * 64)
+        return remote(dp.at[k, 1 - core, some], dr.at[k, some], dr_s.at[k], dr_r.at[k], mate)
+
+    def down_parts(k):
+        first, count = step_blocks(k)
+
+        def part(n):
+            if n == 0:
+                for pos in range(first, first + count):
+                    hx_copy(pos, h2.at[pos, x_other]).wait_recv()
+            c, cols = n // 2, slice(n % 2 * 256, n % 2 * 256 + 256)
+            left = h1[first : first + count].reshape(count * 64, C1)
+            right = h2[first : first + count].reshape(count * 64, C2)
+            dp[k, c, : count * 64, cols] = jnp.dot(
+                left, down_w[c, :C1, cols], preferred_element_type=F32
+            ) + jnp.dot(right, down_w[c, C1:, cols], preferred_element_type=F32)
+            if n == 3:
+                mate_sums(k).start()
+                sent.append(mate_sums(k))
+
+        return [functools.partial(part, n) for n in range(4)]
 
     def return_copy(pos, owner):
         return remote(ds_send.at[pos], fr.at[g], fr_s.at[pos], fr_r.at[g], (owner, b))
 
     returns = []
 
-    def return_step(k):
-        first, count = (0, 1) if k == 0 else (2 * k - 1, 2 if k < 4 else 1)
-        some = pl.ds(0, count * 64)
-        remote(dp.at[k, 1 - core, some], dr.at[k, some], dr_s.at[k], dr_r.at[k], mate).wait_recv()
-        for j in range(count):
+    def return_parts(k):
+        first, count = step_blocks(k)
+
+        def part(j):
+            if j == 0:
+                mate_sums(k).wait_recv()
             pos = first + j
             there = count - 1 - j
             total = (
@@ -368,6 +469,8 @@
             @pl.when(owner == g)
             def _():
                 fr[g] = total
+
+        return [functools.partial(part, j) for j in range(count)]
 
     forward(2, 0)
     forward(0, 0)
@@ -380,18 +483,20 @@
     hx_copy(8, h1.at[0, x_other]).wait_recv()
     forward(1, 0)
     for k in range(1, 5):
-        for kind in (2, 0, 1):
-            for pos in (2 * k - 1, 2 * k) if k < 4 else (7,):
-                hz_copy(kind, pos, pos, ahead).wait_recv()
-                forward(kind, pos)
-                if kind == 2:
-                    to_xmate(pos)
+        parts = down_parts(k - 1)
         if k >= 2:
-            return_step(k - 2)
-        down_step(k - 1)
-    return_step(3)
-    down_step(4)
-    return_step(4)
+            parts = return_parts(k - 2) + parts
+        arrivals = [(kind, pos) for kind in (2, 0, 1) for pos in ((2 * k - 1, 2 * k) if k < 4 else (7,))]
+        for n, (kind, pos) in enumerate(arrivals):
+            hz_copy(kind, pos, pos, ahead).wait_recv()
+            forward(kind, pos)
+            if kind == 2:
+                to_xmate(pos)
+            due = (n + 1) * len(parts) // len(arrivals) - n * len(parts) // len(arrivals)
+            for part in parts[n * len(parts) // len(arrivals) :][:due]:
+                part()
+    for part in return_parts(3) + down_parts(4) + return_parts(4):
+        part()
 
     total = wide_s[...]
     for n in ORDER:
@@ -404,8 +509,8 @@
 
     for copy in merges + gathers + to_mate:
         copy.wait_send()
-    for s in range(4):
-        xg_copy(s).wait_send()
+    for n in range(8):
+        xg_copy(n).wait_send()
     xu_copy.wait_send()
     for copy in sent:
         copy.wait_send()
@@ -416,13 +521,18 @@
             return_copy(pos, owner).wait_send()
 
 
-def feed_forward(w_in, st_in, res, gain, gate, up, down):
+def layer(queries, keys, values, key_new, value_new, lengths, res, gain, gate, up, down):
     vmem = pl.BlockSpec(memory_space=pltpu.VMEM)
     hbm = pl.BlockSpec(memory_space=pl.ANY)
     V = pltpu.VMEM
     dma = lambda *shape: pltpu.SemaphoreType.DMA(shape)
     scratch = [
-        V((4, 64, FEAT), BF16), V((4, 64, 128), F32), V((64, FEAT), F32), V((2, 32, FEAT), BF16),
+        V((64, 2048), BF16), V((64, 64, 128), BF16), V((64, 64, 128), BF16),
+        V((64, 128), BF16), V((64, 128), BF16), pltpu.SMEM((64,), jnp.int32),
+        V((64, FEAT), BF16), V((FEAT,), BF16),
+        V((64, 2048), F32), V((64, 128), F32), V((64, 128), F32), V((16, 64, 128), F32),
+        V((128, 128), F32), V((4, 4, 64, 128), BF16), V((32, 128), F32),
+        V((4, 4, 64, 128), BF16), V((128, 128), F32), V((64, FEAT), F32), V((2, 32, FEAT), BF16),
         V((2, 8, FEAT), F32),
         V((2 * FEAT, HALF), BF16), V((2 * FEAT, HALF), BF16), V((2, HALF, FEAT), BF16),
         V((8, 2, 32, 2 * FEAT), BF16), V((8, 2, 32, WIDE), F32), V((8, 2, 32, HALF), F32),
@@ -435,24 +545,24 @@
         V((8, 2, 32, C1), BF16), V((8, 2, 32, C2), BF16),
         V((5, 2, 128, FEAT), F32), V((5, 128, FEAT), F32),
         V((8, 64, FEAT), BF16), V((8, 64, FEAT), BF16),
-        dma(3), dma(4), dma(4), dma(8), dma(8), dma(8), dma(8), dma(8), dma(8),
-        dma(4), dma(4), dma(4, 2), dma(4, 2), dma(3, 2), dma(3, 2),
+        dma(8), dma(3), dma(4), dma(4), dma(8), dma(8), dma(8), dma(8), dma(8), dma(8),
+        dma(8), dma(8), dma(4, 2), dma(4, 2), dma(3, 2), dma(3, 2),
         dma(4), dma(4), dma(3), dma(3), pltpu.SemaphoreType.DMA, pltpu.SemaphoreType.DMA,
         dma(3, 8), dma(3, 8), dma(9), dma(9), dma(5), dma(5), dma(8), dma(8),
     ]
     return pl.pallas_call(
         kernel,
-        out_shape=jax.ShapeDtypeStruct((64, FEAT), F32),
-        in_specs=[vmem, vmem, vmem, vmem, hbm, hbm, hbm],
+        out_shape=pltpu.VMEM((64, FEAT), F32),
+        in_specs=[hbm] * 11,
         out_specs=vmem,
         scratch_shapes=scratch,
         compiler_params=pltpu.CompilerParams(
-            collective_id=0, has_side_effects=True, vmem_limit_bytes=50 * 1024 * 1024
+            collective_id=0, has_side_effects=True, vmem_limit_bytes=61 * 1024 * 1024
         ),
         cost_estimate=pl.CostEstimate(
             flops=5_300_000_000, bytes_accessed=11_000_000, transcendentals=100_000
         ),
-    )(w_in, st_in, res, gain, gate, up, down)
+    )(queries, keys, values, key_new, value_new, lengths, res, gain, gate, up, down)
 
 
 def on_device(
@@ -468,49 +578,18 @@
     up_weight,
     down_weight,
 ):
-    cycle_size = lax.axis_size("blk")
-    quarters = cycle_size // KV_HEADS
-    per_kv = HEADS // KV_HEADS
-    own_heads = HEADS // cycle_size
-    head_size = key_cache.shape[3]
-    seq_rows = residual_in.shape[0]
-    positions_here = key_cache.shape[2]
-    blk_index = lax.axis_index("blk")
-    kv_head = blk_index // quarters
-    quarter = blk_index % quarters
-    score_scale = 1.0 / math.sqrt(head_size)
-    group_queries = lax.dynamic_slice_in_dim(
-        queries, kv_head * per_kv * head_size, per_kv * head_size, 1
-    )
-    group_queries = group_queries.astype(F32).reshape(seq_rows, per_kv, head_size)
-    fresh_key = lax.dynamic_slice_in_dim(key_new, kv_head * head_size, head_size, 1).astype(F32)
-    fresh_value = lax.dynamic_slice_in_dim(value_new, kv_head * head_size, head_size, 1).astype(F32)
-    keys_here = key_cache[:, 0].astype(F32)
-    values_here = value_cache[:, 0].astype(F32)
-    scores = jnp.einsum("shd,spd->shp", group_queries, keys_here) * score_scale
-    fresh_scores = jnp.einsum("shd,sd->sh", group_queries, fresh_key) * score_scale
-    places = quarter * positions_here + jnp.arange(positions_here, dtype=jnp.int32)
-    usable = (places[None, :] < lengths[:, None])[:, None, :]
-    with_fresh = quarter == 0
-    largest = jnp.maximum(
-        jnp.max(jnp.where(usable, scores, -1e30), axis=2),
-        jnp.where(with_fresh, fresh_scores, -1e30),
-    )
-    weights = jnp.where(usable, jnp.exp(scores - largest[..., None]), 0.0)
-    fresh_weight = jnp.where(with_fresh, jnp.exp(fresh_scores - largest), 0.0)
-    totals = jnp.sum(weights, axis=2) + fresh_weight
-    weighted = (
-        jnp.einsum("shp,spd->shd", weights, values_here)
-        + fresh_weight[..., None] * fresh_value[:, None, :]
-    )
-    w_in = weighted.astype(BF16).reshape(seq_rows, quarters, own_heads * head_size).transpose(1, 0, 2)
-    stats = jnp.concatenate(
-        [largest.reshape(seq_rows, quarters, own_heads), totals.reshape(seq_rows, quarters, own_heads)],
-        axis=2,
-    )
-    st_in = jnp.pad(stats, ((0, 0), (0, 0), (0, 128 - 2 * own_heads))).transpose(1, 0, 2)
-    return feed_forward(
-        w_in, st_in, residual_in, ffn_gain.reshape(1, FEAT), gate_weight, up_weight, down_weight
+    return layer(
+        queries,
+        key_cache,
+        value_cache,
+        key_new,
+        value_new,
+        lengths,
+        residual_in,
+        ffn_gain,
+        gate_weight,
+        up_weight,
+        down_weight,
     )
 
 

time: 96.9 us -> 89 us (0.918)
  matrix products: 3.92 us -> 0 us
  local copies, waits for them, and re-layouts: 4.49 us -> 0.66 us
  Pallas kernels: 85.6 us -> 88.2 us
  other arithmetic: 2.03 us -> 0 us
    dot_general x3 -> x0, matrix products: 3.92 us -> none  [the longest x1 1.99 us: on_device(): scores = jnp.einsum('shd,spd->shp', group_queries, keys_here) * score_scale]
    unnamed x11 -> x1, local copies, waits for them, and re-layouts: 3.38 us -> 0.66 us
    pallas_call x1, Pallas kernels: 85.6 us -> 88.2 us  [layer(): pl.pallas_call(kernel, out_shape=pltpu.VMEM((64, FEAT), F32), in_specs=[h...]
where the time goes in v2:
time: 89 us; the launch traced here: 88.9 us
  Pallas kernels  88.2 us (99%)
    pallas_call x1, Pallas kernels, layer(): pl.pallas_call(kernel, out_shape=pltpu.VMEM((64, FEAT), F32), in_specs=[h...  88.2 us

profile of v2, /device:TPU:7, one launch (start us, length us, event | category | flops | bytes accessed | tf_op | source)
XLA Modules:
  0.0 88.9 jit_solution(2111312238705084436)
XLA Ops:
  0.0 88.2 %shard_map.109 = f32[64,512]{1,0:T(8,128)S(1)} custom-call(bf16[64,16384]{1,0:T(8,128)(2,1)} %queries.1, bf16[64,1,64,128]{3,2,1,0:T(8,128)(2,1)} %keys.1, bf16[64,1,64,128]{3,2,1,0:T(8,128)(2,1)} %values.1, bf16[64,1024]{1,0:T(8,128)(2,1)} %key_new.1, bf16[64,1024]{1,0:T(8,128)(2,1)} %value_new.1, s32[64]{0:T(128)} %lengths.1, bf16[64,512]{1,0:T(8,128)(2,1)} %res_in.1, ...), custom_call_target="tpu_custom_call" | custom-call | flops 5299999744 | bytes 11000000 | tf_op jit(solution)/shard_map/pallas_call | solution.py:553
  88.2 0.7 copy.13

commit v3 on v2

--- a/solution.py
+++ b/solution.py
@@ -19,7 +19,10 @@
 GROUPS = 8
 FEAT = 512
 HALF = 1664
-WIDE = HALF + 128
+TAIL = 384
+UP = HALF - TAIL
+WIDE = UP + 128
+GATE = HALF + TAIL
 C1 = 768
 C2 = HALF - C1
 
@@ -64,6 +67,7 @@
         return (lax.rem(g // 4 + n // 4, 2)) * 4 + lax.rem(g % 4 - n % 4 + 4, 4)
 
     ORDER = (1, 3, 2, 4, 5, 7, 6)
+    FAR_FIRST = (6, 5, 7, 4, 2, 1, 3)
 
     mine = pl.ds(pl.multiple_of(core * HALF, 128), HALF)
     other = pl.ds(pl.multiple_of((1 - core) * HALF, 128), HALF)
@@ -201,7 +205,7 @@
     lanes = pl.ds(pl.multiple_of(core * FEAT, FEAT), FEAT)
     own_slot, own_mate_slot = slots(g)
     gathers = []
-    for n in ORDER[::-1]:
+    for n in FAR_FIRST:
         gathers.append(
             remote(token_s, x_s.at[own_slot, :, :, lanes], tok_s.at[n], tok_r.at[n], (peer(n), b))
         )
@@ -210,7 +214,7 @@
     x_s[own_slot, :, :, lanes] = token_s[...]
     to_mate = [remote(token_s, x_s.at[own_mate_slot, :, :, lanes], mate_s.at[0], mate_r.at[0], mate)]
     to_mate[0].start()
-    for n in ORDER:
+    for n in FAR_FIRST:
         here, there = slots(source(n))
         remote(
             token_s, x_s.at[here, :, :, lanes], tok_s.at[n], tok_r.at[n], (peer(n), b)
@@ -229,8 +233,8 @@
 
     def up_first(lanes_of, add):
         tokens = x_s[pl.ds(0, 2), :, :, lanes_of].reshape(128, FEAT)
-        for lo in range(0, HALF, 512):
-            hi = min(lo + 512, HALF)
+        for lo in range(0, UP, 512):
+            hi = min(lo + 512, UP)
             part = jnp.dot(tokens, up_w[lanes_of, lo:hi], preferred_element_type=F32)
             part = part.reshape(2, 2, 32, hi - lo)
             pu[0:2, :, :, lo:hi] = pu[0:2, :, :, lo:hi] + part if add else part
@@ -249,8 +253,8 @@
 
     def up_pair(s):
         tokens = project(s)
-        for lo in range(0, HALF, 512):
-            hi = min(lo + 512, HALF)
+        for lo in range(0, UP, 512):
+            hi = min(lo + 512, UP)
             part = jnp.dot(tokens, up_w[:, lo:hi], preferred_element_type=F32)
             pu[pl.ds(s * 2, 2), :, :, lo:hi] = part.reshape(2, 2, 32, hi - lo)
         square_sums(s)
@@ -262,7 +266,7 @@
         ]
         squares = plain[0] * plain[0] + plain[1] * plain[1]
         total = jnp.sum(squares, axis=1, keepdims=True)
-        pu[pl.ds(s * 2, 2), :, :, HALF:] = jnp.broadcast_to(total, (128, 128)).reshape(2, 2, 32, 128)
+        pu[pl.ds(s * 2, 2), :, :, UP:] = jnp.broadcast_to(total, (128, 128)).reshape(2, 2, 32, 128)
 
     def gate_pair(s):
         tokens = project(s)
@@ -270,25 +274,27 @@
             hi = min(lo + 512, HALF)
             part = jnp.dot(tokens, gate_w[:, lo:hi], preferred_element_type=F32)
             pg[pl.ds(s * 2, 2), :, :, lo:hi] = part.reshape(2, 2, 32, hi - lo)
+        part = jnp.dot(tokens, up_w[:, UP:], preferred_element_type=F32)
+        pg[pl.ds(s * 2, 2), :, :, HALF:] = part.reshape(2, 2, 32, TAIL)
         xg_send[pl.ds(s * 2, 2)] = pg[pl.ds(s * 2, 2), x_other].astype(BF16)
 
     def xg_copy(n):
         return remote(xg_send.at[n], xg_recv.at[n], xg_ss.at[n], xg_rs.at[n], xmate)
 
     def up_sum(block, half, arrived):
-        body = pu[block, half, :, :HALF]
-        squares = pu[block, half, :, HALF:]
+        body = pu[block, half, :, :UP]
+        squares = pu[block, half, :, UP:]
         for ref in arrived:
-            body = body + ref[:, :HALF].astype(F32)
-            halves = ref[:, HALF:].astype(F32)
+            body = body + ref[:, :UP].astype(F32)
+            halves = ref[:, UP:].astype(F32)
             squares = squares + halves + pltpu.roll(halves, 64, 1)
         return body, squares
 
     def put_up(ref, body, squares):
-        ref[:, :HALF] = body.astype(BF16)
+        ref[:, :UP] = body.astype(BF16)
         high = squares.astype(BF16)
         low = (squares - high.astype(F32)).astype(BF16)
-        ref[:, HALF:] = jnp.where(lane < 64, high.astype(F32), low.astype(F32)).astype(BF16)
+        ref[:, UP:] = jnp.where(lane < 64, high.astype(F32), low.astype(F32)).astype(BF16)
 
     halves = (x_other, x)
     sent = []
@@ -307,22 +313,21 @@
     def gb_copy(s):
         return remote(gb_send.at[s], gb_recv.at[s], gb_ss.at[s], gb_rs.at[s], behind)
 
-    def up_step(s):
-        for n in range(2):
-            h = halves[n]
+    def up_step(s, n):
+        h = halves[n]
+        if s > 0:
+            ua_copy(s - 1, n).wait_recv()
+        arrived = [ua_recv.at[s - 1, h]] if s > 0 else []
+        put_up(ua_send.at[s, h], *up_sum(2 * s, h, arrived))
+        ua_copy(s, n).start()
+        sent.append(ua_copy(s, n))
+        if s < 3:
             if s > 0:
-                ua_copy(s - 1, n).wait_recv()
-            arrived = [ua_recv.at[s - 1, h]] if s > 0 else []
-            put_up(ua_send.at[s, h], *up_sum(2 * s, h, arrived))
-            ua_copy(s, n).start()
-            sent.append(ua_copy(s, n))
-            if s < 3:
-                if s > 0:
-                    ub_copy(s - 1, n).wait_recv()
-                arrived = [ub_recv.at[s - 1, h]] if s > 0 else []
-                put_up(ub_send.at[s, h], *up_sum(2 * s + 1, h, arrived))
-                ub_copy(s, n).start()
-                sent.append(ub_copy(s, n))
+                ub_copy(s - 1, n).wait_recv()
+            arrived = [ub_recv.at[s - 1, h]] if s > 0 else []
+            put_up(ub_send.at[s, h], *up_sum(2 * s + 1, h, arrived))
+            ub_copy(s, n).start()
+            sent.append(ub_copy(s, n))
 
     def gate_step(s):
         xg_copy(2 * s).wait_recv()
@@ -345,24 +350,31 @@
             gb_copy(s).start()
             sent.append(gb_copy(s))
 
-    square_sums(0)
-    up_step(0)
-    gate_pair(0)
-    xg_copy(0).start()
-    xg_copy(1).start()
-
-    def pairs(s, carry):
+    def gate_out(s):
         gate_pair(s)
         xg_copy(2 * s).start()
         xg_copy(2 * s + 1).start()
-        up_pair(s)
-        return carry
-
-    lax.fori_loop(1, 4, pairs, 0)
+
+    square_sums(0)
+    up_step(0, 0)
+    up_step(0, 1)
+    gate_out(0)
+    gate_out(1)
+    up_pair(1)
+    up_step(1, 0)
+    gate_out(2)
     gate_step(0)
-    for s in range(1, 4):
-        up_step(s)
-        gate_step(s)
+    up_step(1, 1)
+    up_pair(2)
+    up_step(2, 0)
+    gate_out(3)
+    gate_step(1)
+    up_pair(3)
+    up_step(2, 1)
+    up_step(3, 0)
+    gate_step(2)
+    up_step(3, 1)
+    gate_step(3)
 
     xu_copy = remote(xu_send, xu_recv, xu_ss, xu_rs, xmate)
     for n in range(2):
@@ -374,8 +386,8 @@
             put_up(xu_send, body, squares)
             xu_copy.start()
         else:
-            pu[7, h, :, :HALF] = body
-            pu[7, h, :, HALF:] = squares
+            pu[7, h, :, :UP] = body
+            pu[7, h, :, UP:] = squares
     xg_copy(7).wait_recv()
     ga_copy(3).wait_recv()
     gb_copy(2).wait_recv()
@@ -383,7 +395,8 @@
     xu_copy.wait_recv()
     up_total, squares = up_sum(7, x, [xu_recv])
     scale = lax.rsqrt(squares[:, 0:1] / D + 1e-05)
-    gate_sum = gate_sum * scale
+    up_total = jnp.concatenate([up_total, gate_sum[:, HALF:]], axis=1)
+    gate_sum = gate_sum[:, :HALF] * scale
     hidden = (gate_sum / (1.0 + jnp.exp(-gate_sum)) * (up_total * scale)).astype(BF16)
     h1[0, x] = hidden[:, :C1]
     h2[0, x] = hidden[:, C1:]
@@ -495,7 +508,7 @@
             due = (n + 1) * len(parts) // len(arrivals) - n * len(parts) // len(arrivals)
             for part in parts[n * len(parts) // len(arrivals) :][:due]:
                 part()
-    for part in return_parts(3) + down_parts(4) + return_parts(4):
+    for part in down_parts(4) + return_parts(3) + return_parts(4):
         part()
 
     total = wide_s[...]
@@ -535,12 +548,12 @@
         V((4, 4, 64, 128), BF16), V((128, 128), F32), V((64, FEAT), F32), V((2, 32, FEAT), BF16),
         V((2, 8, FEAT), F32),
         V((2 * FEAT, HALF), BF16), V((2 * FEAT, HALF), BF16), V((2, HALF, FEAT), BF16),
-        V((8, 2, 32, 2 * FEAT), BF16), V((8, 2, 32, WIDE), F32), V((8, 2, 32, HALF), F32),
-        V((8, 32, HALF), BF16), V((8, 32, HALF), BF16),
+        V((8, 2, 32, 2 * FEAT), BF16), V((8, 2, 32, WIDE), F32), V((8, 2, 32, GATE), F32),
+        V((8, 32, GATE), BF16), V((8, 32, GATE), BF16),
         V((4, 2, 32, WIDE), BF16), V((4, 2, 32, WIDE), BF16),
         V((3, 2, 32, WIDE), BF16), V((3, 2, 32, WIDE), BF16),
-        V((4, 32, HALF), BF16), V((4, 32, HALF), BF16),
-        V((3, 32, HALF), BF16), V((3, 32, HALF), BF16),
+        V((4, 32, GATE), BF16), V((4, 32, GATE), BF16),
+        V((3, 32, GATE), BF16), V((3, 32, GATE), BF16),
         V((32, WIDE), BF16), V((32, WIDE), BF16),
         V((8, 2, 32, C1), BF16), V((8, 2, 32, C2), BF16),
         V((5, 2, 128, FEAT), F32), V((5, 128, FEAT), F32),

time: 89 us -> 85.3 us (0.958)
  Pallas kernels: 88.2 us -> 84.5 us
    pallas_call x1, Pallas kernels: 88.2 us -> 84.5 us  [layer(): pl.pallas_call(kernel, out_shape=pltpu.VMEM((64, FEAT), F32), in_specs=[h...]
where the time goes in v3:
time: 85.3 us; the launch traced here: 85.2 us
  Pallas kernels  84.5 us (99%)
    pallas_call x1, Pallas kernels, layer(): pl.pallas_call(kernel, out_shape=pltpu.VMEM((64, FEAT), F32), in_specs=[h...  84.5 us

profile of v3, /device:TPU:7, one launch (start us, length us, event | category | flops | bytes accessed | tf_op | source)
XLA Modules:
  0.0 85.2 jit_solution(11045202975404356157)
XLA Ops:
  0.0 84.5 %shard_map.109 = f32[64,512]{1,0:T(8,128)S(1)} custom-call(bf16[64,16384]{1,0:T(8,128)(2,1)} %queries.1, bf16[64,1,64,128]{3,2,1,0:T(8,128)(2,1)} %keys.1, bf16[64,1,64,128]{3,2,1,0:T(8,128)(2,1)} %values.1, bf16[64,1024]{1,0:T(8,128)(2,1)} %key_new.1, bf16[64,1024]{1,0:T(8,128)(2,1)} %value_new.1, s32[64]{0:T(128)} %lengths.1, bf16[64,512]{1,0:T(8,128)(2,1)} %res_in.1, ...), custom_call_target="tpu_custom_call" | custom-call | flops 5299999744 | bytes 11000000 | tf_op jit(solution)/shard_map/pallas_call | solution.py:566
  84.6 0.7 copy.13

commit v4 on v3

--- a/solution.py
+++ b/solution.py
@@ -40,7 +40,7 @@
     h1, h2, dp, dr, ds_send, fr,
     load_sem, local_sem, wsem_s, wsem_r, at_s, at_r, tok_s, tok_r, mate_s, mate_r,
     xg_ss, xg_rs, ua_ss, ua_rs, ub_ss, ub_rs, ga_ss, ga_rs, gb_ss, gb_rs, xu_ss, xu_rs,
-    hz_s, hz_r, hx_s, hx_r, dr_s, dr_r, fr_s, fr_r,
+    hz_s, hz_r, hx_s, hx_r, dr_s, dr_r, fr_s, fr_r, fl_s, fl_r,
 ):
     g = lax.axis_index("grp")
     b = lax.axis_index("blk")
@@ -485,6 +485,60 @@
 
         return [functools.partial(part, j) for j in range(count)]
 
+    own_rows = [pl.ds(pl.multiple_of(h * 32, 32), 32) for h in (x, x_other)]
+
+    def owner_of(k, j):
+        return lax.rem(z + (-sign if j == 0 else sign) * k + RING, RING)
+
+    def half_sums(k, n):
+        size = step_blocks(k)[1] * 32
+        some = pl.ds(n * size, size)
+        sem = 2 * k - 3 + n
+        return remote(dp.at[k, 1 - core, some], dr.at[k, some], dr_s.at[sem], dr_r.at[sem], mate)
+
+    def half_copy(k, j, n, slot):
+        pos = 2 * k - 1 + j
+        return remote(
+            ds_send.at[pos, own_rows[n]],
+            fr.at[slot, own_rows[n]],
+            fl_s.at[pos - 5, n],
+            fl_r.at[n, slot],
+            (owner_of(k, j), b),
+        )
+
+    def half_down(k, n):
+        first, count = step_blocks(k)
+        h = (x, x_other)[n]
+        if n == 1:
+            for pos in range(first, first + count):
+                hx_copy(pos, h2.at[pos, x_other]).wait_recv()
+        left = h1[first : first + count, h].reshape(count * 32, C1)
+        right = h2[first : first + count, h].reshape(count * 32, C2)
+        for c in range(2):
+            dp[k, c, n * count * 32 : (n + 1) * count * 32] = jnp.dot(
+                left, down_w[c, :C1], preferred_element_type=F32
+            ) + jnp.dot(right, down_w[c, C1:], preferred_element_type=F32)
+        half_sums(k, n).start()
+        sent.append(half_sums(k, n))
+
+    def half_return(k, n):
+        half_sums(k, n).wait_recv()
+        first, count = step_blocks(k)
+        for j in range(count):
+            here = (n * count + j) * 32
+            there = (n * count + count - 1 - j) * 32
+            total = (dp[k, core, here : here + 32] + dr[k, there : there + 32]).astype(BF16)
+            ds_send[first + j, own_rows[n]] = total
+            owner = owner_of(k, j)
+
+            @pl.when(owner != g)
+            def _():
+                half_copy(k, j, n, g).start()
+
+            @pl.when(owner == g)
+            def _():
+                fr[g, own_rows[n]] = total
+
     forward(2, 0)
     forward(0, 0)
     copy = hx_copy(8, h1.at[0, x])
@@ -495,27 +549,51 @@
     loads[2].wait()
     hx_copy(8, h1.at[0, x_other]).wait_recv()
     forward(1, 0)
-    for k in range(1, 5):
+    for k in range(1, 4):
         parts = down_parts(k - 1)
         if k >= 2:
             parts = return_parts(k - 2) + parts
-        arrivals = [(kind, pos) for kind in (2, 0, 1) for pos in ((2 * k - 1, 2 * k) if k < 4 else (7,))]
+        arrivals = [(kind, pos) for kind in (2, 0, 1) for pos in (2 * k - 1, 2 * k)]
         for n, (kind, pos) in enumerate(arrivals):
             hz_copy(kind, pos, pos, ahead).wait_recv()
             forward(kind, pos)
             if kind == 2:
                 to_xmate(pos)
-            due = (n + 1) * len(parts) // len(arrivals) - n * len(parts) // len(arrivals)
-            for part in parts[n * len(parts) // len(arrivals) :][:due]:
+            lo, hi = n * len(parts) // len(arrivals), (n + 1) * len(parts) // len(arrivals)
+            for part in parts[lo:hi]:
                 part()
-    for part in down_parts(4) + return_parts(3) + return_parts(4):
+    half_down(3, 0)
+    hz_copy(2, 7, 7, ahead).wait_recv()
+    to_xmate(7)
+    for part in return_parts(2):
         part()
+    half_return(3, 0)
+    hz_copy(0, 7, 7, ahead).wait_recv()
+    half_down(4, 0)
+    half_down(3, 1)
+    half_return(4, 0)
+    hz_copy(1, 7, 7, ahead).wait_recv()
+    half_return(3, 1)
+    half_down(4, 1)
+    half_return(4, 1)
 
     total = wide_s[...]
-    for n in ORDER:
-        remote(
-            ds_send.at[0], fr.at[source(n)], fr_s.at[0], fr_r.at[source(n)], (peer(n), b)
-        ).wait_recv()
+    away = lax.rem(z - g + RING, RING)
+    in_halves = (away >= 3) & (away <= 5)
+
+    @pl.when(in_halves)
+    def _():
+        for half in range(2):
+            for n in ORDER:
+                half_copy(4, 0, half, source(n)).wait_recv()
+
+    @pl.when(jnp.logical_not(in_halves))
+    def _():
+        for n in ORDER:
+            remote(
+                ds_send.at[0], fr.at[source(n)], fr_s.at[0], fr_r.at[source(n)], (peer(n), b)
+            ).wait_recv()
+
     for j in range(GROUPS):
         total = total + fr[j].astype(F32)
     out[...] = total
@@ -527,6 +605,13 @@
     xu_copy.wait_send()
     for copy in sent:
         copy.wait_send()
+    for k, j in ((3, 0), (3, 1), (4, 0)):
+
+        @pl.when(owner_of(k, j) != g)
+        def _():
+            half_copy(k, j, 0, g).wait_send()
+            half_copy(k, j, 1, g).wait_send()
+
     for pos, owner in returns:
 
         @pl.when(owner != g)
@@ -561,7 +646,7 @@
         dma(8), dma(3), dma(4), dma(4), dma(8), dma(8), dma(8), dma(8), dma(8), dma(8),
         dma(8), dma(8), dma(4, 2), dma(4, 2), dma(3, 2), dma(3, 2),
         dma(4), dma(4), dma(3), dma(3), pltpu.SemaphoreType.DMA, pltpu.SemaphoreType.DMA,
-        dma(3, 8), dma(3, 8), dma(9), dma(9), dma(5), dma(5), dma(8), dma(8),
+        dma(3, 8), dma(3, 8), dma(9), dma(9), dma(7), dma(7), dma(8), dma(8), dma(3, 2), dma(2, 8),
     ]
     return pl.pallas_call(
         kernel,

time: 85.3 us -> 83.6 us (0.980)
  Pallas kernels: 84.5 us -> 82.9 us
    pallas_call x1, Pallas kernels: 84.5 us -> 82.9 us  [layer(): pl.pallas_call(kernel, out_shape=pltpu.VMEM((64, FEAT), F32), in_specs=[h...]
where the time goes in v4:
time: 83.6 us
  Pallas kernels  82.9 us (99%)
    pallas_call x1, Pallas kernels, layer(): pl.pallas_call(kernel, out_shape=pltpu.VMEM((64, FEAT), F32), in_specs=[h...  82.9 us

profile of v4, /device:TPU:7, one launch (start us, length us, event | category | flops | bytes accessed | tf_op | source)
XLA Modules:
  0.0 83.6 jit_solution(16625364159454228794)
XLA Ops:
  0.0 82.9 %shard_map.109 = f32[64,512]{1,0:T(8,128)S(1)} custom-call(bf16[64,16384]{1,0:T(8,128)(2,1)} %queries.1, bf16[64,1,64,128]{3,2,1,0:T(8,128)(2,1)} %keys.1, bf16[64,1,64,128]{3,2,1,0:T(8,128)(2,1)} %values.1, bf16[64,1024]{1,0:T(8,128)(2,1)} %key_new.1, bf16[64,1024]{1,0:T(8,128)(2,1)} %value_new.1, s32[64]{0:T(128)} %lengths.1, bf16[64,512]{1,0:T(8,128)(2,1)} %res_in.1, ...), custom_call_target="tpu_custom_call" | custom-call | flops 5299999744 | bytes 11000000 | tf_op jit(solution)/shard_map/pallas_call | solution.py:651
  82.9 0.7 copy.13

commit v5 on v4

--- a/solution.py
+++ b/solution.py
@@ -19,7 +19,7 @@
 GROUPS = 8
 FEAT = 512
 HALF = 1664
-TAIL = 384
+TAIL = 512
 UP = HALF - TAIL
 WIDE = UP + 128
 GATE = HALF + TAIL

time: 83.6 us -> 83.6 us (level)
  no operation moved by 1% of the time
where the time goes in v5:
time: 83.6 us; the launch traced here: 83.4 us
  Pallas kernels  82.7 us (99%)
    pallas_call x1, Pallas kernels, layer(): pl.pallas_call(kernel, out_shape=pltpu.VMEM((64, FEAT), F32), in_specs=[h...  82.7 us

profile of v5, /device:TPU:7, one launch (start us, length us, event | category | flops | bytes accessed | tf_op | source)
XLA Modules:
  0.0 83.4 jit_solution(10942045320646650562)
XLA Ops:
  0.0 82.7 %shard_map.109 = f32[64,512]{1,0:T(8,128)S(1)} custom-call(bf16[64,16384]{1,0:T(8,128)(2,1)} %queries.1, bf16[64,1,64,128]{3,2,1,0:T(8,128)(2,1)} %keys.1, bf16[64,1,64,128]{3,2,1,0:T(8,128)(2,1)} %values.1, bf16[64,1024]{1,0:T(8,128)(2,1)} %key_new.1, bf16[64,1024]{1,0:T(8,128)(2,1)} %value_new.1, s32[64]{0:T(128)} %lengths.1, bf16[64,512]{1,0:T(8,128)(2,1)} %res_in.1, ...), custom_call_target="tpu_custom_call" | custom-call | flops 5299999744 | bytes 11000000 | tf_op jit(solution)/shard_map/pallas_call | solution.py:651
  82.7 0.7 copy.13
